TPU v7x, 512 devices: a whole 4x4x16 slice. The times are simulated.
512 devices in a mesh: img: 8 (over x, core), cls: 8 (over z_lo), tpl: 8 (over z_hi, y).
Axes of the slice: x: 4, y: 4, z: 16 (z_hi: 2, z_lo: 8; z = z_hi * 8 + z_lo), core: 2. Of those that a mesh axis runs over, the one named last changes fastest.
Arguments:
- images: bfloat16 [16384, 1280], P(('img', 'tpl')), may hold values from -5 to 5
- labels: int32 [16384], P(('img', 'tpl')), may hold values from 0 to 4095
- templates: bfloat16 [32, 4096, 1280], P('tpl', ('cls', 'img')), may hold values from -0.125 to 0.125
- projection: bfloat16 [1280, 1280], P('img', 'cls'), may hold values from -0.08441157 to 0.08441157
Outputs:
- grad_templates: bfloat16 [32, 4096, 1280], P('tpl', ('cls', 'img'))
- grad_projection: float32 [1280, 1280], P('img', 'cls')
All inputs are finite; a program needn't handle non-finite values.
Results may differ from a plain program's by a relative error of at most 0.011.
Values may be sent and summed in bfloat16 or wider, within the bound.
A program may use at most 64 MiB of HBM per device.

v0:
```python
import jax
import jax.numpy as jnp
from jax import lax
from jax.sharding import PartitionSpec as P

logit_scale = 50.0
epsilon = 1e-06


def inverse_norm(values):
    return lax.rsqrt(jnp.sum(values * values, axis=-1, keepdims=True) + epsilon)


def body(images, labels, templates, projection):
    tpl_count = templates.shape[0]
    cls_count = templates.shape[1]
    feat_width = templates.shape[2]
    tpl_total = tpl_count * lax.axis_size("tpl")
    img_count = lax.axis_size("img")
    wide_proj = lax.all_gather(projection, "cls", axis=1, tiled=True)
    full_proj = lax.all_gather(wide_proj, "img", axis=0, tiled=True)
    flat_tpl = templates.reshape(tpl_count * cls_count, feat_width)
    text_z = jnp.dot(flat_tpl, full_proj, preferred_element_type=jnp.float32)
    text_rz = inverse_norm(text_z)
    text_u = text_z * text_rz
    u_three = text_u.reshape(tpl_count, cls_count, feat_width)
    local_sum = jnp.sum(u_three, axis=0)
    mean_emb = lax.psum(local_sum, "tpl") / tpl_total
    mean_rn = inverse_norm(mean_emb)
    class_w = mean_emb * mean_rn
    class_b = class_w.astype(jnp.bfloat16)
    img_f = images.astype(jnp.float32)
    img_b = (img_f * inverse_norm(img_f)).astype(jnp.bfloat16)
    all_img, all_labels = (
        lax.all_gather(img_b, "img", axis=0, tiled=True),
        lax.all_gather(labels, "img", axis=0, tiled=True),
    )
    scores = logit_scale * jnp.einsum(
        "cd,nd->cn", class_b, all_img, preferred_element_type=jnp.float32
    )
    exp_scores = jnp.exp(scores)
    totals = lax.psum(jnp.sum(exp_scores, axis=0), ("img", "cls"))
    first_id = (lax.axis_index("cls") * img_count + lax.axis_index("img")) * cls_count
    class_ids = first_id + lax.broadcasted_iota(jnp.int32, (cls_count, 1), 0)
    one_hot = (all_labels[None, :] == class_ids).astype(jnp.float32)
    grad_logit = (exp_scores / totals[None, :] - one_hot).astype(jnp.bfloat16)
    partial_value = logit_scale * jnp.dot(grad_logit, all_img, preferred_element_type=jnp.float32)
    class_g = lax.psum(partial_value, "tpl")
    dot_wg = jnp.sum(class_w * class_g, axis=1, keepdims=True)
    grad_mean = (class_g - class_w * dot_wg) * mean_rn
    per_u = grad_mean / tpl_total
    inner_prod = jnp.sum(u_three * per_u[None], axis=2, keepdims=True)
    grad_z = (
        (per_u[None] - u_three * inner_prod) * text_rz.reshape(tpl_count, cls_count, 1)
    ).astype(jnp.bfloat16)
    grad_flat = grad_z.reshape(tpl_count * cls_count, feat_width)
    grad_tpl = lax.dot_general(
        grad_flat, full_proj, (((1,), (1,)), ((), ())), preferred_element_type=jnp.float32
    )
    grad_templates = grad_tpl.astype(jnp.bfloat16).reshape(tpl_count, cls_count, feat_width)
    tpl_columns = lax.all_to_all(flat_tpl, "img", split_axis=1, concat_axis=0, tiled=True)
    partial_proj = lax.dot_general(
        tpl_columns,
        lax.all_gather(grad_flat, "img", axis=0, tiled=True),
        (((0,), (0,)), ((), ())),
        preferred_element_type=jnp.float32,
    )
    shared_proj = lax.psum_scatter(
        partial_proj.astype(jnp.bfloat16), "cls", scatter_dimension=1, tiled=True
    )
    grad_projection = lax.psum(shared_proj, "tpl").astype(jnp.float32)
    return (grad_templates, grad_projection)


def solution(mesh):
    in_specs = (
        P(("img", "tpl"), None),
        P(("img", "tpl")),
        P("tpl", ("cls", "img"), None),
        P("img", "cls"),
    )
    out_specs = (P("tpl", ("cls", "img"), None), P("img", "cls"))
    return jax.shard_map(body, mesh=mesh, in_specs=in_specs, out_specs=out_specs, check_vma=False)
```

profile of v0, /device:TPU:6, one launch (start us, length us, event | category | flops | bytes accessed | tf_op | source)
XLA Modules:
  0.0 856.8 jit_solution(12290353934308617125)
XLA Ops:
  7.2 1.0 copy.10
  8.3 51.1 %all_gather.15 = bf16[160,1280]{0,1:T(8,128)(2,1)S(1)} all-gather(bf16[160,160]{0,1:T(8,128)(2,1)S(1)} %copy.10), channel_id=1, replica_groups=mesh['img'=8,'cls'=8,'tpl'=8] {'cls'}, dimensions={1}, use_global_device_ids=true | all-gather | bytes 460800 | tf_op jit(solution)/shard_map/all_gather | solution.py:20
  59.4 1.0 copy.11
  60.5 0.2 fusion.2
  60.7 36.6 %all-gather.5.cloned.1.call-done = bf16[1280,1280]{1,0:T(8,128)(2,1)} async-done(((bf16[160,1280]{1,0:T(8,128)(2,1)}), bf16[1280,1280]{1,0:T(8,128)(2,1)}) %all-gather.5.cloned.1.call-update) | async-done | bytes 3276816 | tf_op jit(solution)/shard_map/all_gather | solution.py:21
  97.3 3.0 multiply_reduce_fusion
  100.4 0.2 broadcast_multiply_fusion
  100.6 0.8 reduce_sum.64
  101.5 1.0 fusion.3
  102.6 8.4 all-gather
  111.0 144.2 %all-reduce.3.cloned.1.call-done = f32[64,1280]{1,0:T(8,128)} async-done(((f32[64,1280]{1,0:T(8,128)}), f32[64,1280]{1,0:T(8,128)}) %all-reduce.3.cloned.1.call-update) | async-done | bytes 327696 | tf_op jit(solution)/shard_map/psum | solution.py:28
  255.2 1.1 multiply_reduce_fusion.2
  256.3 34.3 %all-gather.7.cloned.1.call-done = bf16[2048,1280]{1,0:T(8,128)(2,1)} async-done(((bf16[256,1280]{1,0:T(8,128)(2,1)}), bf16[2048,1280]{1,0:T(8,128)(2,1)}) %all-gather.7.cloned.1.call-update) | async-done | bytes 5242896 | tf_op jit(solution)/shard_map/all_gather | solution.py:35
  290.6 4.3 fusion.11
  294.9 204.1 %psum.29 = f32[2048]{0:T(1024)S(1)} all-reduce(f32[2048]{0:T(1024)S(1)} %get-tuple-element.6), channel_id=1, replica_groups=mesh['img'=8,'cls'=8,'tpl'=8] {'img','cls'}, use_global_device_ids=true, to_apply=%region_6.0 | all-reduce | flops 2048 | bytes 16384 | tf_op jit(solution)/shard_map/psum | solution.py:42
  499.1 4.3 convolution_multiply_fusion
  503.5 164.7 %all-reduce.5.cloned.1.call-done = f32[64,1280]{1,0:T(8,128)} async-done(((f32[64,1280]{1,0:T(8,128)}), f32[64,1280]{1,0:T(8,128)}) %all-reduce.5.cloned.1.call-update) | async-done | bytes 327696 | tf_op jit(solution)/shard_map/psum | solution.py:48
  668.1 1.2 multiply_reduce_fusion.1
  669.3 1.1 multiply_multiply_fusion
  670.4 0.3 fusion.4
  670.7 1.1 fusion.6
  671.9 1.3 all_to_all.14
  673.2 1.0 copy.12
  674.2 20.7 %all_to_all.19 = bf16[256,8,160]{0,2,1:T(8,128)(2,1)S(1)} all-to-all(bf16[256,8,160]{0,2,1:T(8,128)(2,1)S(1)} %copy.12), channel_id=1, replica_groups=mesh['img'=8,'cls'=8,'tpl'=8] {'img'}, dimensions={1} | all-to-all | bytes 1310720 | tf_op jit(solution)/shard_map/all_to_all | solution.py:61
  695.0 15.7 %all-gather.9.cloned.1.call-done = bf16[2048,1280]{1,0:T(8,128)(2,1)} async-done(((bf16[256,1280]{1,0:T(8,128)(2,1)}), bf16[2048,1280]{1,0:T(8,128)(2,1)}) %all-gather.9.cloned.1.call-update) | async-done | bytes 5242896 | tf_op jit(solution)/shard_map/all_gather | solution.py:64
  710.7 3.5 fusion
  714.2 1.1 copy.14
  715.3 3.8 convolution_convert_fusion
  719.1 57.3 %reduce-scatter.4.cloned.1.call-done = bf16[160,160]{1,0:T(8,128)(2,1)} async-done(((bf16[1280,160]{1,0:T(8,128)(2,1)}), bf16[160,160]{1,0:T(8,128)(2,1)}) %reduce-scatter.4.cloned.1.call-update) | async-done | bytes 51216
  776.4 1.0 copy.15
  777.4 71.8 %psum.31 = bf16[160,160]{1,0:T(8,128)(2,1)S(1)} all-reduce(bf16[160,160]{1,0:T(8,128)(2,1)S(1)} %copy.15), channel_id=1, replica_groups=mesh['img'=8,'cls'=8,'tpl'=8] {'tpl'}, use_global_device_ids=true, to_apply=%region_11.0 | all-reduce | flops 25600 | bytes 102400 | tf_op jit(solution)/shard_map/psum | solution.py:71
  849.3 0.7 convert_element_type.40
  (29 shorter events, 0.5 us)
Async XLA Ops:
  7.2 53.3 %copy-start.1 = (bf16[256,1280]{1,0:T(8,128)(2,1)S(1)}, bf16[256,1280]{1,0:T(8,128)(2,1)}, u32[]{:S(2)}) copy-start(bf16[256,1280]{1,0:T(8,128)(2,1)} %param.4) | copy-start | bytes 1966084
  7.2 90.2 %all-gather.5.cloned.1.call-start = ((), (), s32[]{:S(2)}) async-start(), calls=%async_computation.2 | async-start | bytes 3686400 | tf_op jit(solution)/shard_map/all_gather | solution.py:21
  8.3 89.1 %copy-start.3 = (bf16[4,64,1280]{2,1,0:T(8,128)(2,1)S(1)}, bf16[4,64,1280]{2,1,0:T(8,128)(2,1)}, u32[]{:S(2)}) copy-start(bf16[4,64,1280]{2,1,0:T(8,128)(2,1)} %param.6) | copy-start | bytes 1966084
  60.4 194.7 %all-reduce.3.cloned.1.call-start = ((), (), s32[]{:S(2)}) async-start(), calls=%async_computation.3 | async-start | bytes 655360 | tf_op jit(solution)/shard_map/psum | solution.py:28
  101.4 1.2 copy-start.5
  101.4 189.1 %all-gather.7.cloned.1.call-start = ((), (), s32[]{:S(2)}) async-start(), calls=%async_computation.4 | async-start | bytes 5898240 | tf_op jit(solution)/shard_map/all_gather | solution.py:35
  102.5 565.6 %all-reduce.5.cloned.1.call-start = ((), (), s32[]{:S(2)}) async-start(), calls=%async_computation.5 | async-start | bytes 655360 | tf_op jit(solution)/shard_map/psum | solution.py:48
  499.1 169.1 %copy-start = (f32[64,1280]{1,0:T(8,128)S(1)}, f32[64,1280]{1,0:T(8,128)}, u32[]{:S(2)}) copy-start(f32[64,1280]{1,0:T(8,128)} %all-reduce.3.cloned.1.call-done) | copy-start | bytes 983044
  503.4 207.3 %all-gather.9.cloned.1.call-start = ((), (), s32[]{:S(2)}) async-start(), calls=%async_computation.6 | async-start | bytes 5898240 | tf_op jit(solution)/shard_map/all_gather | solution.py:64
  670.7 1.2 copy-start.4
  671.9 104.6 %reduce-scatter.4.cloned.1.call-start = ((), (), s32[]{:S(2)}) async-start(), calls=%async_computation.7 | async-start | bytes 737280
  714.2 1.1 copy-start.2
Sparse Core Ops, SparseCore 0:
  60.5 36.7 all-gather.4
  101.5 153.5 all-reduce.2
  258.1 32.4 all-gather.6
  503.5 164.5 all-reduce.4
  672.0 38.6 all-gather.8
  715.4 60.9 reduce-scatter.3
where the time goes:
time: 857 us
  waiting for transfers between devices  453 us (53%)
  blocking collectives  356 us (42%)
  matrix products  19 us (2%)
  between operations  14.3 us (2%)
    psum x1, blocking collectives, body(): totals = lax.psum(jnp.sum(exp_scores, axis=0), ('img', 'cls'))  204 us
    psum x1, waiting for transfers between devices, body(): class_g = lax.psum(partial_value, 'tpl')  165 us
    psum x1, waiting for transfers between devices, body(): mean_emb = lax.psum(local_sum, 'tpl') / tpl_total  144 us
    psum x1, blocking collectives, body(): grad_projection = lax.psum(shared_proj, 'tpl').astype(jnp.float32)  71.8 us
    unnamed x7, waiting for transfers between devices  57.4 us
    all_gather x1, blocking collectives, body(): wide_proj = lax.all_gather(projection, 'cls', axis=1, tiled=True)  51.1 us
    all_gather x1, waiting for transfers between devices, body(): full_proj = lax.all_gather(wide_proj, 'img', axis=0, tiled=True)  36.6 us
    all_gather x1, waiting for transfers between devices, body(): lax.all_gather(img_b, 'img', axis=0, tiled=True)  34.3 us
  transfers between devices with their start and end apart: 6, of which 6 were waited for; matrix products, arithmetic and copies ran while one was open for 1% of the time, Pallas kernels for 0%

commit v1 on v0

--- a/solution.py
+++ b/solution.py
@@ -2,6 +2,7 @@
 import jax.numpy as jnp
 from jax import lax
 from jax.sharding import PartitionSpec as P
+from jax.lax import psum
 
 logit_scale = 50.0
 epsilon = 1e-06
@@ -39,7 +40,9 @@
         "cd,nd->cn", class_b, all_img, preferred_element_type=jnp.float32
     )
     exp_scores = jnp.exp(scores)
-    totals = lax.psum(jnp.sum(exp_scores, axis=0), ("img", "cls"))
+    totals = jnp.sum(exp_scores, axis=0)
+    for j0 in ("img", "cls"):
+        totals = psum(totals, j0)
     first_id = (lax.axis_index("cls") * img_count + lax.axis_index("img")) * cls_count
     class_ids = first_id + lax.broadcasted_iota(jnp.int32, (cls_count, 1), 0)
     one_hot = (all_labels[None, :] == class_ids).astype(jnp.float32)

time: 857 us -> 682 us (0.80)
  blocking collectives: 356 us -> 198 us
  waiting for transfers between devices: 453 us -> 436 us
    psum x1 -> x2, blocking collectives: 204 us -> 45.7 us  [body(): totals = psum(totals, j0)]
    psum x1, waiting for transfers between devices: 165 us -> 148 us  [body(): class_g = lax.psum(partial_value, 'tpl')]
where the time goes in v1:
time: 682 us; the launch traced here: 681 us
  waiting for transfers between devices  436 us (64%)
  blocking collectives  198 us (29%)
  matrix products  19 us (3%)
  between operations  14.3 us (2%)
  other arithmetic  7.75 us (1%)
    psum x1, waiting for transfers between devices, body(): class_g = lax.psum(partial_value, 'tpl')  148 us
    psum x1, waiting for transfers between devices, body(): mean_emb = lax.psum(local_sum, 'tpl') / tpl_total  144 us
    psum x1, blocking collectives, body(): grad_projection = lax.psum(shared_proj, 'tpl').astype(jnp.float32)  71.6 us
    unnamed x7, waiting for transfers between devices  57.4 us
    all_gather x1, blocking collectives, body(): wide_proj = lax.all_gather(projection, 'cls', axis=1, tiled=True)  51.1 us
    psum x2, blocking collectives, body(): totals = psum(totals, j0)  45.7 us
    all_gather x1, waiting for transfers between devices, body(): full_proj = lax.all_gather(wide_proj, 'img', axis=0, tiled=True)  36.6 us
    all_gather x1, waiting for transfers between devices, body(): lax.all_gather(img_b, 'img', axis=0, tiled=True)  34.3 us
  transfers between devices with their start and end apart: 6, of which 6 were waited for; matrix products, arithmetic and copies ran while one was open for 1% of the time, Pallas kernels for 0%

profile of v1, /device:TPU:6, one launch (start us, length us, event | category | flops | bytes accessed | tf_op | source)
XLA Modules:
  0.0 681.0 jit_solution(14284836278866557815)
XLA Ops:
  7.2 1.0 copy.10
  8.3 51.1 %all_gather.15 = bf16[160,1280]{0,1:T(8,128)(2,1)S(1)} all-gather(bf16[160,160]{0,1:T(8,128)(2,1)S(1)} %copy.10), channel_id=1, replica_groups=mesh['img'=8,'cls'=8,'tpl'=8] {'cls'}, dimensions={1}, use_global_device_ids=true | all-gather | bytes 460800 | tf_op jit(solution)/shard_map/all_gather | solution.py:21
  59.4 1.0 copy.11
  60.5 0.2 fusion.2
  60.7 36.6 %all-gather.5.cloned.1.call-done = bf16[1280,1280]{1,0:T(8,128)(2,1)} async-done(((bf16[160,1280]{1,0:T(8,128)(2,1)}), bf16[1280,1280]{1,0:T(8,128)(2,1)}) %all-gather.5.cloned.1.call-update) | async-done | bytes 3276816 | tf_op jit(solution)/shard_map/all_gather | solution.py:22
  97.3 3.0 multiply_reduce_fusion
  100.6 0.8 reduce_sum.64
  101.5 1.0 fusion.3
  102.6 8.4 %all-gather = s32[8,1,256]{2,1,0:T(1,128)S(1)} all-gather(s32[1,1,256]{2,1,0:T(1,128)S(1)} %bitcast.36), channel_id=1, replica_groups=mesh['img'=8,'cls'=8,'tpl'=8] {'img'}, dimensions={0}, use_global_device_ids=true | all-gather | bytes 9216 | tf_op jit(solution)/shard_map/all_gather | solution.py:37
  111.0 144.2 %all-reduce.3.cloned.1.call-done = f32[64,1280]{1,0:T(8,128)} async-done(((f32[64,1280]{1,0:T(8,128)}), f32[64,1280]{1,0:T(8,128)}) %all-reduce.3.cloned.1.call-update) | async-done | bytes 327696 | tf_op jit(solution)/shard_map/psum | solution.py:29
  255.2 1.1 multiply_reduce_fusion.2
  256.3 34.3 %all-gather.7.cloned.1.call-done = bf16[2048,1280]{1,0:T(8,128)(2,1)} async-done(((bf16[256,1280]{1,0:T(8,128)(2,1)}), bf16[2048,1280]{1,0:T(8,128)(2,1)}) %all-gather.7.cloned.1.call-update) | async-done | bytes 5242896 | tf_op jit(solution)/shard_map/all_gather | solution.py:36
  290.6 4.3 fusion.11
  294.9 11.6 %psum.36 = f32[2048]{0:T(1024)S(1)} all-reduce(f32[2048]{0:T(1024)S(1)} %get-tuple-element.6), channel_id=1, replica_groups=mesh['img'=8,'cls'=8,'tpl'=8] {'img'}, use_global_device_ids=true, to_apply=%region_6.0 | all-reduce | flops 2048 | bytes 16384 | tf_op jit(solution)/shard_map/psum | solution.py:45
  306.5 34.1 %psum.37 = f32[2048]{0:T(1024)S(1)} all-reduce(f32[2048]{0:T(1024)S(1)} %psum.36), channel_id=1, replica_groups=mesh['img'=8,'cls'=8,'tpl'=8] {'cls'}, use_global_device_ids=true, to_apply=%region_7.0 | all-reduce | flops 2048 | bytes 16384 | tf_op jit(solution)/shard_map/psum | solution.py:45
  340.6 4.3 convolution_multiply_fusion
  345.0 147.5 %all-reduce.5.cloned.1.call-done = f32[64,1280]{1,0:T(8,128)} async-done(((f32[64,1280]{1,0:T(8,128)}), f32[64,1280]{1,0:T(8,128)}) %all-reduce.5.cloned.1.call-update) | async-done | bytes 327696 | tf_op jit(solution)/shard_map/psum | solution.py:51
  492.5 1.2 multiply_reduce_fusion.1
  493.7 1.1 multiply_multiply_fusion
  494.8 0.3 fusion.4
  495.1 1.1 fusion.6
  496.3 1.3 all_to_all.14
  497.7 1.0 copy.12
  498.7 20.7 %all_to_all.19 = bf16[256,8,160]{0,2,1:T(8,128)(2,1)S(1)} all-to-all(bf16[256,8,160]{0,2,1:T(8,128)(2,1)S(1)} %copy.12), channel_id=1, replica_groups=mesh['img'=8,'cls'=8,'tpl'=8] {'img'}, dimensions={1} | all-to-all | bytes 1310720 | tf_op jit(solution)/shard_map/all_to_all | solution.py:64
  519.4 15.7 %all-gather.9.cloned.1.call-done = bf16[2048,1280]{1,0:T(8,128)(2,1)} async-done(((bf16[256,1280]{1,0:T(8,128)(2,1)}), bf16[2048,1280]{1,0:T(8,128)(2,1)}) %all-gather.9.cloned.1.call-update) | async-done | bytes 5242896 | tf_op jit(solution)/shard_map/all_gather | solution.py:67
  535.1 3.5 fusion
  538.6 1.1 copy.14
  539.7 3.8 convolution_convert_fusion
  543.6 57.3 %reduce-scatter.4.cloned.1.call-done = bf16[160,160]{1,0:T(8,128)(2,1)} async-done(((bf16[1280,160]{1,0:T(8,128)(2,1)}), bf16[160,160]{1,0:T(8,128)(2,1)}) %reduce-scatter.4.cloned.1.call-update) | async-done | bytes 51216
  600.9 1.0 copy.15
  601.9 71.6 %psum.39 = bf16[160,160]{1,0:T(8,128)(2,1)S(1)} all-reduce(bf16[160,160]{1,0:T(8,128)(2,1)S(1)} %copy.15), channel_id=1, replica_groups=mesh['img'=8,'cls'=8,'tpl'=8] {'tpl'}, use_global_device_ids=true, to_apply=%region_12.0 | all-reduce | flops 25600 | bytes 102400 | tf_op jit(solution)/shard_map/psum | solution.py:74
  673.5 0.7 convert_element_type.40
  (30 shorter events, 0.6 us)
Async XLA Ops:
  7.2 53.3 %copy-start.1 = (bf16[256,1280]{1,0:T(8,128)(2,1)S(1)}, bf16[256,1280]{1,0:T(8,128)(2,1)}, u32[]{:S(2)}) copy-start(bf16[256,1280]{1,0:T(8,128)(2,1)} %param.4) | copy-start | bytes 1966084
  7.2 90.2 %all-gather.5.cloned.1.call-start = ((), (), s32[]{:S(2)}) async-start(), calls=%async_computation.2 | async-start | bytes 3686400 | tf_op jit(solution)/shard_map/all_gather | solution.py:22
  8.3 89.1 %copy-start.3 = (bf16[4,64,1280]{2,1,0:T(8,128)(2,1)S(1)}, bf16[4,64,1280]{2,1,0:T(8,128)(2,1)}, u32[]{:S(2)}) copy-start(bf16[4,64,1280]{2,1,0:T(8,128)(2,1)} %param.6) | copy-start | bytes 1966084
  60.4 194.7 %all-reduce.3.cloned.1.call-start = ((), (), s32[]{:S(2)}) async-start(), calls=%async_computation.3 | async-start | bytes 655360 | tf_op jit(solution)/shard_map/psum | solution.py:29
  101.4 1.2 copy-start.5
  101.4 189.1 %all-gather.7.cloned.1.call-start = ((), (), s32[]{:S(2)}) async-start(), calls=%async_computation.4 | async-start | bytes 5898240 | tf_op jit(solution)/shard_map/all_gather | solution.py:36
  102.5 390.0 %all-reduce.5.cloned.1.call-start = ((), (), s32[]{:S(2)}) async-start(), calls=%async_computation.5 | async-start | bytes 655360 | tf_op jit(solution)/shard_map/psum | solution.py:51
  340.6 151.9 %copy-start = (f32[64,1280]{1,0:T(8,128)S(1)}, f32[64,1280]{1,0:T(8,128)}, u32[]{:S(2)}) copy-start(f32[64,1280]{1,0:T(8,128)} %all-reduce.3.cloned.1.call-done) | copy-start | bytes 983044
  345.0 190.1 %all-gather.9.cloned.1.call-start = ((), (), s32[]{:S(2)}) async-start(), calls=%async_computation.6 | async-start | bytes 5898240 | tf_op jit(solution)/shard_map/all_gather | solution.py:67
  495.1 1.2 copy-start.4
  496.3 104.6 %reduce-scatter.4.cloned.1.call-start = ((), (), s32[]{:S(2)}) async-start(), calls=%async_computation.7 | async-start | bytes 737280
  538.6 1.1 copy-start.2
Sparse Core Ops, SparseCore 0:
  60.5 36.7 all-gather.4
  101.5 153.5 all-reduce.2
  258.1 32.4 all-gather.6
  345.1 147.3 all-reduce.4
  496.4 38.6 all-gather.8
  539.9 60.9 reduce-scatter.3
